TPU v7x, 32 devices: a whole 2x2x4 slice. The times are simulated.
32 devices in a mesh: groups: 2 (over x), dp: 16 (over z, y, core).
Axes of the slice: x: 2, y: 2, z: 4, core: 2. Of those that a mesh axis runs over, the one named last changes fastest.
Arguments:
- tokens: bfloat16 [768, 8192], P(('groups', 'dp')), parts along dimension 0, may hold values from -6 to 6
- block_job: int32 [96], P('groups'), parts along dimension 0, may hold values from 0 to 15
- source: int32 [32], P('groups'), parts along dimension 0, may hold values from 0 to 47, as said below
- adapter_home: int32 [32], P('groups'), parts along dimension 0, may hold values from 0 to 15, each once
- up_weight: bfloat16 [8192, 28672], P(None, 'dp'), may hold values from -0.0625 to 0.0625
- adapter_a: bfloat16 [32, 8192, 16], P(('groups', 'dp')), parts along dimension 0, may hold values from -0.0625 to 0.0625
- adapter_b: bfloat16 [32, 16, 28672], P('groups', None, 'dp'), parts along dimension 0, may hold values from -1.5 to 1.5
- cotangent: bfloat16 [256, 28672], P('groups', 'dp'), parts along dimension 0, may hold values from -0.125 to 0.125
Outputs:
- mixed: bfloat16 [256, 28672], P('groups', 'dp'), parts along dimension 0
- grad_a: float32 [32, 8192, 16], P(('groups', 'dp')), parts along dimension 0
- grad_b: float32 [32, 16, 28672], P('groups', None, 'dp'), parts along dimension 0
There are 2 independent parts, one for each index of `groups`. A program takes and returns all parts, laid end to end along the dimension named above; an argument that names none is the same for every part. Nothing has to cross between parts.
Inputs may be any that keep to these rules, and one draw needn't show every extreme that they name: `source`: entries are distinct block slots (device * 3 + k). The blocks a device holds before rebalancing are its slots 0 to c - 1, where c is the number of entries naming that device; c runs from 0 to 3, reaches 3 on some device, and the c sum to 16. Where c > 0, the device's own entry is its slot 0; the devices with c = 0 hold the other blocks.
All inputs are finite; a program needn't handle non-finite values.
Results may differ from a plain program's by a relative error of at most 0.0046.
Values may be sent and summed in bfloat16 or wider, within the bound.
A program may use at most 128 MiB of HBM per device.

v0:
```python
import jax
import jax.numpy as jnp
from jax import lax
from jax.sharding import PartitionSpec as P

HOLD = 3


SCALE = 2.0


def on_device(tokens, block_job, source, adapter_home, up_weight, adapter_a, adapter_b, cotangent):
    devices = lax.axis_size("dp")
    own_index = lax.axis_index("dp")
    width = tokens.shape[1]
    block_rows = tokens.shape[0] // HOLD
    columns = up_weight.shape[1]
    blocks = tokens.reshape(HOLD, block_rows, width)
    every_slot = lax.all_gather(blocks, "dp", axis=0, tiled=True)
    gathered = every_slot[source]
    flat_rows = gathered.reshape(-1, width)
    base_out = jnp.dot(flat_rows, up_weight, preferred_element_type=jnp.float32)
    slot_count = block_job.shape[0]
    job_pick = source[:, None] == jnp.arange(slot_count, dtype=jnp.int32)[None, :]
    job_of_block = jnp.sum(jnp.where(job_pick, block_job[None, :], 0), axis=1)
    job_total = adapter_home.shape[0]
    home_pick = job_of_block[:, None] == jnp.arange(job_total, dtype=jnp.int32)[None, :]
    slot = jnp.sum(jnp.where(home_pick, adapter_home[None, :], 0), axis=1)
    is_home = slot == own_index
    code_term = jnp.einsum(
        "nbd,dr->nbr", gathered, adapter_a[0], preferred_element_type=jnp.float32
    )
    code_term = jnp.where(is_home[:, None, None], code_term, 0.0)
    code_sum = lax.psum(code_term, "dp")
    codes_b = code_sum.astype(jnp.bfloat16)
    factor_b = adapter_b[slot]
    low_rank = jnp.einsum("nbr,nrc->nbc", codes_b, factor_b, preferred_element_type=jnp.float32)
    mixed = (base_out + SCALE * low_rank.reshape(-1, columns)).astype(jnp.bfloat16)
    upstream = cotangent.reshape(devices, block_rows, columns)
    back_term = jnp.einsum("nbc,nrc->nbr", upstream, factor_b, preferred_element_type=jnp.float32)
    back_sum = lax.psum(back_term, "dp")
    back_b = back_sum.astype(jnp.bfloat16)
    per_block_b = jnp.einsum("nbr,nbc->nrc", codes_b, upstream, preferred_element_type=jnp.float32)
    assign = (slot[:, None] == jnp.arange(job_total, dtype=jnp.int32)[None, :]).astype(jnp.float32)
    grad_b = SCALE * jnp.einsum("nj,nrc->jrc", assign, per_block_b, precision=lax.Precision.HIGHEST)
    masked_back = jnp.where(is_home[:, None, None], back_b, jnp.zeros((), jnp.bfloat16))
    grad_local = jnp.einsum(
        "nbd,nbr->dr", gathered, masked_back, preferred_element_type=jnp.float32
    )
    grad_a = SCALE * grad_local[None]
    return (mixed, grad_a, grad_b)


def solution(mesh):
    placed = (
        P(("groups", "dp"), None),
        P("groups"),
        P("groups"),
        P("groups"),
        P(None, "dp"),
        P(("groups", "dp"), None, None),
        P("groups", None, "dp"),
        P("groups", "dp"),
    )
    return jax.shard_map(
        on_device,
        mesh=mesh,
        in_specs=placed,
        out_specs=(P("groups", "dp"), P(("groups", "dp"), None, None), P("groups", None, "dp")),
        check_vma=False,
    )
```

profile of v0, /device:TPU:0, one launch (start us, length us, event | category | flops | bytes accessed | tf_op | source)
XLA Modules:
  0.0 168.9 jit_solution(10626475396283995242)
XLA Ops:
  7.2 0.0 copy-start
  7.2 0.0 copy-start.4
  7.2 0.0 copy-start.2
  7.2 0.0 all-gather.2.cloned.1.call-start
  7.2 0.7 all-gather.2.cloned.1.call-update
  7.9 0.9 select_reduce_fusion.1
  8.8 0.8 select_reduce_fusion
  9.7 0.0 copy-done
  9.7 0.6 gather_fusion.1
  10.3 0.0 copy-done.4
  10.3 0.0 copy-start.1
  10.3 0.0 copy-done.2
  10.3 0.3 convolution_bitcast_fusion.1
  10.7 0.5 copy-done.1
  11.2 63.7 %all-gather.2.cloned.1.call-done = bf16[48,8,8192]{2,1,0:T(8,128)(2,1)} async-done(((bf16[3,8,8192]{2,1,0:T(8,128)(2,1)}), bf16[48,8,8192]{2,1,0:T(8,128)(2,1)}) %all-gather.2.cloned.1.call-update) | async-done | bytes 6291472 | tf_op jit(solution)/shard_map/all_gather | solution.py:19
  74.9 3.5 %gather_fusion = bf16[16,8,8192]{2,1,0:T(8,128)(2,1)S(1)} fusion(bf16[48,8,8192]{2,1,0:T(8,128)(2,1)} %all-gather.2.cloned.1.call-done, s32[1024]{0:T(1024)S(1)} %pad_clamp_fusion.1), kind=kCustom, calls=%fused_computation | custom fusion | bytes 4194368 | tf_op jit(solution)/shard_map/gather | solution.py:20
  78.4 2.3 %convolution_select_fusion = f32[16,8,16]{2,1,0:T(8,128)} fusion(bf16[16,8,8192]{2,1,0:T(8,128)(2,1)S(1)} %gather_fusion, bf16[1,8192,16]{1,2,0:T(8,128)(2,1)} %param.13, pred[16]{0:T(512)(128)(4,1)S(1)} %broadcast_compare_fusion), kind=kOutput, calls=%fused_computation.13 | convolution fusion | flops 33556480 | bytes 2367504 | tf_op jit(solution)/shard_map/nbd,dr->nbr/dot_general | solution.py:30
  80.6 60.8 %all-reduce = (bf16[16,8,16]{2,1,0:T(8,128)(2,1)}, bf16[16,8,16]{2,1,0:T(8,128)(2,1)}) all-reduce(f32[16,8,16]{2,1,0:T(8,128)} %convolution_select_fusion, f32[16,8,16]{2,1,0:T(8,128)S(1)} %convolution_bitcast_fusion.1), channel_id=1, replica_groups=mesh['groups'=2,'dp'=16] {'dp'}, use_global_device_ids=true, to_apply=%region_2.3 | all-reduce | flops 4096 | bytes 24576 | tf_op jit(solution)/shard_map/psum | solution.py:34
  141.5 0.0 copy-start.3
  141.5 1.5 fusion.2
  142.9 1.2 fusion.6
  144.1 0.0 copy-done.3
  144.2 1.3 fusion.1
  145.5 2.0 %convolution_multiply_fusion = f32[16,16,1792]{2,0,1:T(8,128)S(1)} fusion(f32[16,16,1792]{2,1,0:T(8,128)S(1)} %fusion.6, s32[16]{0:T(128)S(1)} %select_reduce_fusion), kind=kOutput, calls=%fused_computation.5 | convolution fusion | flops 88539392 | bytes 3670080 | tf_op jit(solution)/shard_map/nj,nrc->jrc/dot_general | solution.py:45
  147.5 2.3 %copy.20 = f32[16,16,1792]{2,1,0:T(8,128)} copy(f32[16,16,1792]{2,0,1:T(8,128)S(1)} %convolution_multiply_fusion) | data formatting | bytes 3670016
  149.8 12.3 %fusion.3 = bf16[128,1792]{1,0:T(8,128)(2,1)} fusion(f32[128,1792]{1,0:T(8,128)S(1)} %fusion.2, bf16[8192,1792]{1,0:T(8,128)(2,1)} %param.12, bf16[16,8,8192]{2,1,0:T(8,128)(2,1)S(1)} %gather_fusion), kind=kOutput, calls=%fused_computation.9 | convolution fusion | flops 3758555136 | bytes 32833536 | tf_op jit(solution)/shard_map/dot_general | solution.py:22
  (5 shorter events, 0.0 us)
Async XLA Ops:
  7.2 2.5 %copy-start = (bf16[16,16,1792]{2,1,0:T(8,128)(2,1)S(1)}, bf16[16,16,1792]{2,1,0:T(8,128)(2,1)}, u32[]{:S(2)}) copy-start(bf16[16,16,1792]{2,1,0:T(8,128)(2,1)} %param.14) | copy-start | bytes 2752516
  7.2 3.1 %copy-start.4 = (s32[16]{0:T(128)S(1)}, s32[16]{0:T(128)}, u32[]{:S(2)}) copy-start(s32[16]{0:T(128)} %param.10) | copy-start | bytes 196
  7.2 3.1 %copy-start.2 = (bf16[128,1792]{1,0:T(8,128)(2,1)S(1)}, bf16[128,1792]{1,0:T(8,128)(2,1)}, u32[]{:S(2)}) copy-start(bf16[128,1792]{1,0:T(8,128)(2,1)} %param.15) | copy-start | bytes 1376260
  7.2 67.7 %all-gather.2.cloned.1.call-start = ((), (), s32[]{:S(2)}) async-start(), calls=%async_computation | async-start | bytes 6684672 | tf_op jit(solution)/shard_map/all_gather | solution.py:19
  10.3 0.9 copy-start.1
  141.5 2.7 %copy-start.3 = (bf16[16,8,16]{2,1,0:T(8,128)(2,1)S(1)}, bf16[16,8,16]{2,1,0:T(8,128)(2,1)}, u32[]{:S(2)}) copy-start(bf16[16,8,16]{2,1,0:T(8,128)(2,1)} %get-tuple-element.16) | copy-start | bytes 12292
Sparse Core Ops, SparseCore 0:
  10.3 64.5 all-gather.1
where the time goes:
time: 169 us
  waiting for transfers between devices  64.4 us (38%)
  blocking collectives  60.8 us (36%)
  matrix products  20.9 us (12%)
  between operations  14.2 us (8%)
  local copies, waits for them, and re-layouts  6.9 us (4%)
  other arithmetic  1.73 us (1%)
    all_gather x1, waiting for transfers between devices, on_device(): every_slot = lax.all_gather(blocks, 'dp', axis=0, tiled=True)  63.7 us
    psum x1, blocking collectives, on_device(): code_sum = lax.psum(code_term, 'dp')  60.8 us
    dot_general x1, matrix products, on_device(): base_out = jnp.dot(flat_rows, up_weight, preferred_element_type=jnp.float32)  12.3 us
    gather x1, local copies, waits for them, and re-layouts, on_device(): gathered = every_slot[source]  3.46 us
  transfers between devices with their start and end apart: 1, of which 1 were waited for; matrix products, arithmetic and copies ran while one was open for 2% of the time, Pallas kernels for 0%

commit v1 on v0

v1 whole, which is shorter than its diff:
```python
import functools

import jax
import jax.numpy as jnp
from jax import lax
from jax.experimental import pallas as pl
from jax.experimental.pallas import tpu as pltpu
from jax.sharding import PartitionSpec as P

HOLD = 3
SCALE = 2.0
W_PARTS = 8


def dot(a, b, dims=((1,), (0,))):
    return lax.dot_general(a, b, (dims, ((), ())), preferred_element_type=jnp.float32)


def kernel(n, rows_y, rank, source, block_job, adapter_home, tokens, up_weight, adapter_a, adapter_b,
           cotangent, mixed, grad_a, grad_b, weight, factor_a, factor_b, upstream, stage, picked, total, code_acc,
           back_out, back_in, codes, load_sem, stage_send, stage_recv, back_send, back_recv, code_send,
           code_recv, ring_send, ring_recv, pair_send, pair_recv):
    rows, width = cotangent.shape[0], tokens.shape[1]
    blk = rows // n
    chunk = width // n
    chips = n // 2
    half = chips // 2
    length = chips // rows_y
    me = lax.axis_index("dp")
    core = me % 2
    chip = me // 2
    line, depth = chip % rows_y, chip // rows_y
    place = depth + line * (chips - 1 - 2 * depth)
    step = 1 - 2 * core
    sibling = chip * 2 + 1 - core

    def chip_at(position):
        position = (position + 2 * chips) % chips
        turn, along = position // length, position % length
        return (along + turn * (length - 1 - 2 * along)) * rows_y + turn

    following = chip_at(place + step) * 2 + core

    def local(src, dst, index):
        return pltpu.make_async_copy(src, dst, load_sem.at[index])

    def remote(src, dst, sent, got, target):
        return pltpu.make_async_remote_copy(src, dst, sent, got, device_id={"dp": target},
                                            device_id_type=pl.DeviceIdType.MESH)

    barrier = pltpu.get_barrier_semaphore()

    def greet(offset, carry):
        pl.semaphore_signal(barrier, inc=1, device_id={"dp": (me + offset) % n}, device_id_type=pl.DeviceIdType.MESH)
        return carry

    lax.fori_loop(1, n, greet, 0)

    def columns(k):
        return pl.ds(pl.multiple_of(k * chunk, chunk), chunk)

    own = local(tokens.at[:, columns(me)], stage.at[me], 0)
    load_up = local(cotangent, upstream, 1)
    load_b = local(adapter_b, factor_b, 2)
    load_a = local(adapter_a, factor_a, 3)
    share = width // W_PARTS
    load_w = [local(up_weight.at[pl.ds(i * share, share)], weight.at[pl.ds(i * share, share)], 4 + i)
              for i in range(W_PARTS)]
    for copy in (own, load_up, load_b, load_a):
        copy.start()
    pl.semaphore_wait(barrier, n - 1)

    def stage_copy(offset):
        k = (me + offset) % n
        return remote(tokens.at[:, columns(k)], stage.at[me], stage_send.at[offset], stage_recv.at[offset], k)

    def each(body):
        def run(offset, carry):
            body(offset)
            return carry
        lax.fori_loop(1, n, run, 0)

    each(lambda offset: stage_copy(offset).start())
    for copy in load_w:
        copy.start()

    load_up.wait()
    load_b.wait()
    back_out[...] = dot(factor_b[...], upstream[...], ((1,), (1,))).reshape(n, rank, rows)
    back_in[me] = back_out[me]

    def back_copy(offset):
        k = (me + offset) % n
        return remote(back_out.at[k], back_in.at[me], back_send.at[offset], back_recv.at[offset], k)

    lane = lax.broadcasted_iota(jnp.int32, (8, rows), 1) // blk
    slot_of = jnp.zeros((8, rows), jnp.int32)
    row_block = lax.broadcasted_iota(jnp.int32, (rows, 128), 0) // blk
    source_of = jnp.zeros((rows, 128), jnp.int32)
    for e in range(n):
        origin = source[e]
        home = adapter_home[block_job[origin]]
        slot_of = jnp.where(lane == e, home, slot_of)
        source_of = jnp.where(row_block == e, origin, source_of)
    places = n * HOLD * blk
    at = lax.broadcasted_iota(jnp.int32, (rows, places), 1)
    row = lax.broadcasted_iota(jnp.int32, (rows, places), 0)
    wanted = source_of[:, :1] * blk + row % blk
    choose = jnp.where(at == wanted, 1.0, 0.0).astype(jnp.bfloat16)

    own.wait()
    each(lambda offset: stage_copy(offset).wait_recv())
    held = stage[...].astype(jnp.float32).reshape(places, chunk).astype(jnp.bfloat16)
    picked[me] = dot(choose, held).astype(jnp.bfloat16)

    def piece(t, h, away=-1):
        return chip_at(place + away * t * step) * 2 + (core + h) % 2

    def ring(t, h):
        k = piece(t, h)
        return remote(picked.at[k], picked.at[k], ring_send.at[2 * t + h], ring_recv.at[2 * t + h], following)

    def pair(t, h):
        k = piece(t, h)
        return remote(picked.at[k], picked.at[k], pair_send.at[2 * t + h], pair_recv.at[2 * t + h], sibling)

    def use(k):
        part = picked[k]
        total[...] += dot(part, weight[columns(k), :])
        code_acc[...] += dot(factor_a[:, columns(k)], part, ((1,), (1,)))

    pair(0, 0).start()
    ring(0, 0).start()
    each(lambda offset: back_copy(offset).start())
    total[...] = jnp.zeros_like(total)
    code_acc[...] = jnp.zeros_like(code_acc)
    pair(0, 0).wait_recv()
    ring(0, 1).start()
    load_a.wait()
    for copy in load_w:
        copy.wait()
    use(me)
    use(sibling)

    def hop(t, carry):
        for h in range(2):
            ring(t - 1, h).wait_recv()
            pair(t, h).start()
            if h == 0:
                ring(t, 0).start()
            else:
                @pl.when(t < half - 1)
                def _():
                    ring(t, 1).start()
            use(piece(t, h))
        for h in range(2):
            pair(t, h).wait_recv()
            use(piece(t, 1 - h, 1))
        return carry

    lax.fori_loop(1, half, hop, 0)
    ring(half - 1, 0).wait_recv()
    pair(half, 0).start()
    use(piece(half, 0))
    pair(half, 0).wait_recv()
    use(piece(half, 1, 1))

    codes[me] = code_acc[...].astype(jnp.bfloat16)

    def code_copy(offset):
        k = (me + offset) % n
        return remote(codes.at[me], codes.at[me], code_send.at[offset], code_recv.at[offset], k)

    each(lambda offset: code_copy(offset).start())

    each(lambda offset: back_copy(offset).wait_recv())
    back_sum = jnp.sum(back_in[...], axis=0)
    back_b = jnp.where(slot_of[:1] == me, back_sum, 0.0).astype(jnp.bfloat16)
    for k in range(n):
        grad_a[:, k * chunk:(k + 1) * chunk] = SCALE * dot(back_b, picked[k])

    each(lambda offset: code_copy(offset).wait_recv())
    adapter_of = lax.broadcasted_iota(jnp.int32, (n * rank, rows), 0) // rank
    code_rows = codes[...].astype(jnp.float32).reshape(n * rank, rows)
    code_rows = jnp.where(slot_of[:1] == adapter_of, code_rows, 0.0)
    code_b = code_rows.astype(jnp.bfloat16)
    mixed[...] = (total[...] + SCALE * dot(code_rows.T.astype(jnp.bfloat16), factor_b[...])).astype(jnp.bfloat16)
    grad_b[...] = SCALE * dot(code_b, upstream[...])

    each(lambda offset: stage_copy(offset).wait_send())
    each(lambda offset: back_copy(offset).wait_send())
    each(lambda offset: code_copy(offset).wait_send())

    def ended(t, carry):
        ring(t, 0).wait_send()
        pair(t, 0).wait_send()
        return carry

    def ended_other(t, carry):
        ring(t - 1, 1).wait_send()
        pair(t, 1).wait_send()
        return carry

    lax.fori_loop(0, half, ended, 0)
    pair(half, 0).wait_send()
    lax.fori_loop(1, half, ended_other, 0)


def on_device(rows_y, tokens, block_job, source, adapter_home, up_weight, adapter_a, adapter_b, cotangent):
    n = lax.axis_size("dp")
    width = tokens.shape[1]
    rows, hidden = cotangent.shape
    jobs, rank, _ = adapter_b.shape
    chunk = width // n
    smem = pl.BlockSpec(memory_space=pltpu.SMEM)
    anywhere = pl.BlockSpec(memory_space=pl.ANY)
    vmem = pl.BlockSpec(memory_space=pltpu.VMEM)
    bf16, f32 = jnp.bfloat16, jnp.float32
    dma = lambda count: pltpu.SemaphoreType.DMA((count,))
    mixed, grad_a, grad_b = pl.pallas_call(
        functools.partial(kernel, n, rows_y, rank),
        out_shape=(
            jax.ShapeDtypeStruct((rows, hidden), bf16),
            jax.ShapeDtypeStruct((rank, width), f32),
            jax.ShapeDtypeStruct((jobs * rank, hidden), f32),
        ),
        in_specs=[smem] * 3 + [anywhere] * 5,
        out_specs=(vmem,) * 3,
        scratch_shapes=[
            pltpu.VMEM((width, hidden), bf16),
            pltpu.VMEM((rank, width), bf16),
            pltpu.VMEM((jobs * rank, hidden), bf16),
            pltpu.VMEM((rows, hidden), bf16),
            pltpu.VMEM((n,) + (tokens.shape[0], chunk), bf16),
            pltpu.VMEM((n, rows, chunk), bf16),
            pltpu.VMEM((rows, hidden), f32),
            pltpu.VMEM((rank, rows), f32),
            pltpu.VMEM((n, rank, rows), f32),
            pltpu.VMEM((n, rank, rows), f32),
            pltpu.VMEM((n, rank, rows), bf16),
            dma(4 + W_PARTS),
        ] + [dma(n)] * 6 + [dma(n)] * 2 + [dma(n + 2)] * 2,
        compiler_params=pltpu.CompilerParams(
            collective_id=0, has_side_effects=True, vmem_limit_bytes=56 * 1024 * 1024
        ),
    )(
        source, block_job, adapter_home, tokens, up_weight, adapter_a[0].T,
        adapter_b.reshape(jobs * rank, hidden), cotangent,
    )
    return mixed, grad_a.T[None], grad_b.reshape(jobs, rank, hidden)


def solution(mesh):
    placed = (
        P(("groups", "dp"), None),
        P("groups"),
        P("groups"),
        P("groups"),
        P(None, "dp"),
        P(("groups", "dp"), None, None),
        P("groups", None, "dp"),
        P("groups", "dp"),
    )
    rows_y = 2 if mesh.shape["groups"] == 2 else 1
    return jax.shard_map(
        functools.partial(on_device, rows_y),
        mesh=mesh,
        in_specs=placed,
        out_specs=(P("groups", "dp"), P(("groups", "dp"), None, None), P("groups", None, "dp")),
        check_vma=False,
    )
```

time: 169 us -> 49 us (0.29)
  waiting for transfers between devices: 64.4 us -> 0 us
  blocking collectives: 60.8 us -> 0 us
  Pallas kernels: 0 us -> 43.1 us
  matrix products: 20.9 us -> 0 us
  between operations: 14.2 us -> 0.65 us
  local copies, waits for them, and re-layouts: 6.9 us -> 5.05 us
  other arithmetic: 1.73 us -> 0 us
    all_gather x1 -> x0, waiting for transfers between devices: 63.7 us -> none  [on_device(): every_slot = lax.all_gather(blocks, 'dp', axis=0, tiled=True)]
    psum x1 -> x0, blocking collectives: 60.8 us -> none  [on_device(): code_sum = lax.psum(code_term, 'dp')]
    pallas_call x0 -> x1, Pallas kernels: none -> 43.1 us  [on_device(): pl.pallas_call(functools.partial(kernel, n, rows_y, rank), out_shape=(jax...]
    dot_general x7 -> x0, matrix products: 20.9 us -> none  [the longest x1 12.3 us: on_device(): base_out = jnp.dot(flat_rows, up_weight, preferred_element_type=jnp.float32)]
    gather x2 -> x0, local copies, waits for them, and re-layouts: 4.07 us -> none  [the longest x1 3.46 us: on_device(): gathered = every_slot[source]]
    unnamed x11 -> x5, local copies, waits for them, and re-layouts: 2.83 us -> 5.05 us
    reduce_sum x2 -> x0, other arithmetic: 1.69 us -> none  [the longest x1 0.85 us: on_device(): job_of_block = jnp.sum(jnp.where(job_pick, block_job[None, :], 0), axis=1)]
  transfers between devices with their start and end apart: 1 -> 0, of which waited for: 1 -> 0; matrix products, arithmetic and copies ran while one was open for 2% -> 0% of each run, Pallas kernels for 0% -> 0%
where the time goes in v1:
time: 49 us; the launch traced here: 48.8 us
  Pallas kernels  43.1 us (88%)
  local copies, waits for them, and re-layouts  5.05 us (10%)
  between operations  0.65 us (1%)
    pallas_call x1, Pallas kernels, on_device(): pl.pallas_call(functools.partial(kernel, n, rows_y, rank), out_shape=(jax...  43.1 us
    unnamed x5, local copies, waits for them, and re-layouts  5.05 us

profile of v1, /device:TPU:0, one launch (start us, length us, event | category | flops | bytes accessed | tf_op | source)
XLA Modules:
  0.0 48.8 jit_solution(8997461831126119506)
XLA Ops:
  0.6 43.1 %shard_map.103 = (bf16[128,1792]{1,0:T(8,128)(2,1)}, f32[16,8192]{1,0:T(8,128)}, f32[256,1792]{1,0:T(8,128)}) custom-call(s32[16]{0:T(128)} %source.1, s32[48]{0:T(128)} %block_job.1, s32[16]{0:T(128)} %adapter_home.1, bf16[24,8192]{1,0:T(8,128)(2,1)} %tokens.1, bf16[8192,1792]{1,0:T(8,128)(2,1)} %up_weight.1, bf16[16,8192]{1,0:T(8,128)(2,1)} %bitcast.11, ...), custom_call_target="tpu_custom_call" | custom-call | tf_op jit(solution)/shard_map/pallas_call | solution.py:220
  43.7 0.0 copy-start
  43.7 1.9 %copy.14 = bf16[128,1792]{1,0:T(8,128)(2,1)} copy(bf16[128,1792]{1,0:T(8,128)(2,1)} %get-tuple-element.12) | data formatting | bytes 917504
  45.7 1.9 %copy.15 = f32[1,8192,16]{1,2,0:T(8,128)} copy(f32[1,8192,16]{1,2,0:T(8,128)} %bitcast.10) | data formatting | bytes 1048576
  47.6 0.0 copy-done
  47.6 1.2 %copy.16 = f32[16,16,1792]{2,1,0:T(8,128)} copy(f32[16,16,1792]{2,1,0:T(8,128)S(1)} %bitcast.8) | data formatting | bytes 3670016
Async XLA Ops:
  43.7 3.8 %copy-start = (f32[256,1792]{1,0:T(8,128)S(1)}, f32[256,1792]{1,0:T(8,128)}, u32[]{:S(2)}) copy-start(f32[256,1792]{1,0:T(8,128)} %get-tuple-element.8) | copy-start | bytes 5505028

commit v2 on v1

--- a/solution.py
+++ b/solution.py
@@ -10,6 +10,8 @@
 HOLD = 3
 SCALE = 2.0
 W_PARTS = 8
+SPLIT = 2
+OUT_PARTS = 4
 
 
 def dot(a, b, dims=((1,), (0,))):
@@ -17,9 +19,9 @@
 
 
 def kernel(n, rows_y, rank, source, block_job, adapter_home, tokens, up_weight, adapter_a, adapter_b,
-           cotangent, mixed, grad_a, grad_b, weight, factor_a, factor_b, upstream, stage, picked, total, code_acc,
-           back_out, back_in, codes, load_sem, stage_send, stage_recv, back_send, back_recv, code_send,
-           code_recv, ring_send, ring_recv, pair_send, pair_recv):
+           cotangent, total_out, grad_a_out, codes_out, weight, factor_a, factor_b, upstream, stage, picked, total, code_acc,
+           grad_a, code_b, back_out, back_pair, back_in, codes, load_sem, stage_send, stage_recv, back_send, back_recv,
+           code_send, code_recv, ring_send, ring_recv, pair_send, pair_recv):
     rows, width = cotangent.shape[0], tokens.shape[1]
     blk = rows // n
     chunk = width // n
@@ -66,7 +68,7 @@
     share = width // W_PARTS
     load_w = [local(up_weight.at[pl.ds(i * share, share)], weight.at[pl.ds(i * share, share)], 4 + i)
               for i in range(W_PARTS)]
-    for copy in (own, load_up, load_b, load_a):
+    for copy in [own, load_up, load_b, load_a] + load_w:
         copy.start()
     pl.semaphore_wait(barrier, n - 1)
 
@@ -81,17 +83,22 @@
         lax.fori_loop(1, n, run, 0)
 
     each(lambda offset: stage_copy(offset).start())
-    for copy in load_w:
-        copy.start()
 
     load_up.wait()
     load_b.wait()
-    back_out[...] = dot(factor_b[...], upstream[...], ((1,), (1,))).reshape(n, rank, rows)
-    back_in[me] = back_out[me]
+    back_out[...] = dot(factor_b[...], upstream[...], ((1,), (1,))).reshape(chips, 2, rank, rows)
+    back_half = remote(back_out.at[:, 1 - core], back_pair, back_send.at[0], back_recv.at[0], sibling)
+    back_half.start()
 
     def back_copy(offset):
-        k = (me + offset) % n
-        return remote(back_out.at[k], back_in.at[me], back_send.at[offset], back_recv.at[offset], k)
+        to = (chip + offset) % chips
+        return remote(back_out.at[to, core], back_in.at[chip], back_send.at[offset], back_recv.at[offset], to * 2 + core)
+
+    def each_chip(body):
+        def run(offset, carry):
+            body(offset)
+            return carry
+        lax.fori_loop(1, chips, run, 0)
 
     lane = lax.broadcasted_iota(jnp.int32, (8, rows), 1) // blk
     slot_of = jnp.zeros((8, rows), jnp.int32)
@@ -116,53 +123,79 @@
     def piece(t, h, away=-1):
         return chip_at(place + away * t * step) * 2 + (core + h) % 2
 
-    def ring(t, h):
+    cut = rows // SPLIT
+
+    def ring(t, h, i):
         k = piece(t, h)
-        return remote(picked.at[k], picked.at[k], ring_send.at[2 * t + h], ring_recv.at[2 * t + h], following)
-
-    def pair(t, h):
+        at, index = pl.ds(i * cut, cut), (2 * t + h) * SPLIT + i
+        return remote(picked.at[k, at], picked.at[k, at], ring_send.at[index], ring_recv.at[index], following)
+
+    def pair(t, h, i):
         k = piece(t, h)
-        return remote(picked.at[k], picked.at[k], pair_send.at[2 * t + h], pair_recv.at[2 * t + h], sibling)
+        at, index = pl.ds(i * cut, cut), (2 * t + h) * SPLIT + i
+        return remote(picked.at[k, at], picked.at[k, at], pair_send.at[index], pair_recv.at[index], sibling)
 
     def use(k):
         part = picked[k]
         total[...] += dot(part, weight[columns(k), :])
         code_acc[...] += dot(factor_a[:, columns(k)], part, ((1,), (1,)))
 
-    pair(0, 0).start()
-    ring(0, 0).start()
-    each(lambda offset: back_copy(offset).start())
+    for i in range(SPLIT):
+        pair(0, 0, i).start()
+        ring(0, 0, i).start()
     total[...] = jnp.zeros_like(total)
     code_acc[...] = jnp.zeros_like(code_acc)
-    pair(0, 0).wait_recv()
-    ring(0, 1).start()
+    for i in range(SPLIT):
+        pair(0, 0, i).wait_recv()
+        ring(0, 1, i).start()
+    back_half.wait()
+    for c in range(chips):
+        back_out[c, core] = back_out[c, core] + back_pair[c]
+    back_in[chip] = back_out[chip, core]
+    each_chip(lambda offset: back_copy(offset).start())
     load_a.wait()
     for copy in load_w:
         copy.wait()
     use(me)
-    use(sibling)
-
-    def hop(t, carry):
-        for h in range(2):
-            ring(t - 1, h).wait_recv()
-            pair(t, h).start()
+
+    def forward(t, h):
+        for i in range(SPLIT):
+            ring(t - 1, h, i).wait_recv()
+            pair(t, h, i).start()
             if h == 0:
-                ring(t, 0).start()
+                ring(t, 0, i).start()
             else:
                 @pl.when(t < half - 1)
                 def _():
-                    ring(t, 1).start()
-            use(piece(t, h))
+                    ring(t, 1, i).start()
+
+    def hop(t, carry):
+        forward(t, 0)
+        use(jnp.where(t == 1, sibling, piece(t - 1, 1)))
+        forward(t, 1)
+        use(piece(t, 0))
+
+        @pl.when(t > 1)
+        def _():
+            for h in range(2):
+                for i in range(SPLIT):
+                    pair(t - 1, h, i).wait_recv()
+                use(piece(t - 1, 1 - h, 1))
+        return carry
+
+    lax.fori_loop(1, half, hop, 0)
+    for i in range(SPLIT):
+        ring(half - 1, 0, i).wait_recv()
+        pair(half, 0, i).start()
+    use(sibling if half == 1 else piece(half - 1, 1))
+    use(piece(half, 0))
+    if half > 1:
         for h in range(2):
-            pair(t, h).wait_recv()
-            use(piece(t, 1 - h, 1))
-        return carry
-
-    lax.fori_loop(1, half, hop, 0)
-    ring(half - 1, 0).wait_recv()
-    pair(half, 0).start()
-    use(piece(half, 0))
-    pair(half, 0).wait_recv()
+            for i in range(SPLIT):
+                pair(half - 1, h, i).wait_recv()
+            use(piece(half - 1, 1 - h, 1))
+    for i in range(SPLIT):
+        pair(half, 0, i).wait_recv()
     use(piece(half, 1, 1))
 
     codes[me] = code_acc[...].astype(jnp.bfloat16)
@@ -173,37 +206,76 @@
 
     each(lambda offset: code_copy(offset).start())
 
-    each(lambda offset: back_copy(offset).wait_recv())
+    store_total = local(total, total_out, 0)
+    store_total.start()
+    each_chip(lambda offset: back_copy(offset).wait_recv())
     back_sum = jnp.sum(back_in[...], axis=0)
     back_b = jnp.where(slot_of[:1] == me, back_sum, 0.0).astype(jnp.bfloat16)
     for k in range(n):
         grad_a[:, k * chunk:(k + 1) * chunk] = SCALE * dot(back_b, picked[k])
-
+    store_a = local(grad_a, grad_a_out, 1)
+    store_a.start()
+
+    adapter_of = lax.broadcasted_iota(jnp.int32, (n * rank, rows), 0) // rank
     each(lambda offset: code_copy(offset).wait_recv())
-    adapter_of = lax.broadcasted_iota(jnp.int32, (n * rank, rows), 0) // rank
     code_rows = codes[...].astype(jnp.float32).reshape(n * rank, rows)
-    code_rows = jnp.where(slot_of[:1] == adapter_of, code_rows, 0.0)
-    code_b = code_rows.astype(jnp.bfloat16)
-    mixed[...] = (total[...] + SCALE * dot(code_rows.T.astype(jnp.bfloat16), factor_b[...])).astype(jnp.bfloat16)
-    grad_b[...] = SCALE * dot(code_b, upstream[...])
+    code_b[...] = jnp.where(slot_of[:1] == adapter_of, code_rows, 0.0).astype(jnp.bfloat16)
+    store_codes = local(code_b, codes_out, 2)
+    store_codes.start()
 
     each(lambda offset: stage_copy(offset).wait_send())
-    each(lambda offset: back_copy(offset).wait_send())
     each(lambda offset: code_copy(offset).wait_send())
+    each_chip(lambda offset: back_copy(offset).wait_send())
 
     def ended(t, carry):
-        ring(t, 0).wait_send()
-        pair(t, 0).wait_send()
+        for i in range(SPLIT):
+            ring(t, 0, i).wait_send()
+            pair(t, 0, i).wait_send()
         return carry
 
     def ended_other(t, carry):
-        ring(t - 1, 1).wait_send()
-        pair(t, 1).wait_send()
+        for i in range(SPLIT):
+            ring(t - 1, 1, i).wait_send()
+            pair(t, 1, i).wait_send()
         return carry
 
     lax.fori_loop(0, half, ended, 0)
-    pair(half, 0).wait_send()
+    for i in range(SPLIT):
+        pair(half, 0, i).wait_send()
     lax.fori_loop(1, half, ended_other, 0)
+    for copy in (store_total, store_a, store_codes):
+        copy.wait()
+
+
+def finish(total_in, grad_a_in, codes_in, adapter_b, cotangent, mixed_out, grad_a_out, grad_b_out, total, codes,
+           factor_b, upstream, grad_a, mixed, grad_b, sem):
+    def local(src, dst, index):
+        return pltpu.make_async_copy(src, dst, sem.at[index])
+
+    loads = [local(codes_in, codes, 0), local(cotangent, upstream, 1), local(adapter_b, factor_b, 2),
+             local(total_in, total, 3), local(grad_a_in, grad_a, 4)]
+    for copy in loads:
+        copy.start()
+    stores = []
+    loads[0].wait()
+    loads[1].wait()
+    share = grad_b.shape[0] // OUT_PARTS
+    for i in range(OUT_PARTS):
+        at = pl.ds(i * share, share)
+        grad_b[at] = SCALE * dot(codes[at], upstream[...])
+        stores.append(local(grad_b.at[at], grad_b_out.at[at], 7 + i))
+        stores[-1].start()
+    loads[4].wait()
+    stores.append(local(grad_a, grad_a_out, 5))
+    stores[-1].start()
+    loads[2].wait()
+    loads[3].wait()
+    code_rows = codes[...].astype(jnp.float32).T.astype(jnp.bfloat16)
+    mixed[...] = (total[...] + SCALE * dot(code_rows, factor_b[...])).astype(jnp.bfloat16)
+    stores.append(local(mixed, mixed_out, 6))
+    stores[-1].start()
+    for copy in stores:
+        copy.wait()
 
 
 def on_device(rows_y, tokens, block_job, source, adapter_home, up_weight, adapter_a, adapter_b, cotangent):
@@ -212,20 +284,20 @@
     rows, hidden = cotangent.shape
     jobs, rank, _ = adapter_b.shape
     chunk = width // n
+    factor_b = adapter_b.reshape(jobs * rank, hidden)
     smem = pl.BlockSpec(memory_space=pltpu.SMEM)
     anywhere = pl.BlockSpec(memory_space=pl.ANY)
-    vmem = pl.BlockSpec(memory_space=pltpu.VMEM)
     bf16, f32 = jnp.bfloat16, jnp.float32
     dma = lambda count: pltpu.SemaphoreType.DMA((count,))
-    mixed, grad_a, grad_b = pl.pallas_call(
+    base, grad_a, codes = pl.pallas_call(
         functools.partial(kernel, n, rows_y, rank),
         out_shape=(
-            jax.ShapeDtypeStruct((rows, hidden), bf16),
+            jax.ShapeDtypeStruct((rows, hidden), f32),
             jax.ShapeDtypeStruct((rank, width), f32),
-            jax.ShapeDtypeStruct((jobs * rank, hidden), f32),
+            jax.ShapeDtypeStruct((jobs * rank, rows), bf16),
         ),
         in_specs=[smem] * 3 + [anywhere] * 5,
-        out_specs=(vmem,) * 3,
+        out_specs=(anywhere,) * 3,
         scratch_shapes=[
             pltpu.VMEM((width, hidden), bf16),
             pltpu.VMEM((rank, width), bf16),
@@ -235,18 +307,42 @@
             pltpu.VMEM((n, rows, chunk), bf16),
             pltpu.VMEM((rows, hidden), f32),
             pltpu.VMEM((rank, rows), f32),
-            pltpu.VMEM((n, rank, rows), f32),
-            pltpu.VMEM((n, rank, rows), f32),
+            pltpu.VMEM((rank, width), f32),
+            pltpu.VMEM((jobs * rank, rows), bf16),
+            pltpu.VMEM((n // 2, 2, rank, rows), f32),
+            pltpu.VMEM((n // 2, rank, rows), f32),
+            pltpu.VMEM((n // 2, rank, rows), f32),
             pltpu.VMEM((n, rank, rows), bf16),
             dma(4 + W_PARTS),
-        ] + [dma(n)] * 6 + [dma(n)] * 2 + [dma(n + 2)] * 2,
+        ] + [dma(n)] * 2 + [dma(n // 2)] * 2 + [dma(n)] * 2 + [dma(n * SPLIT)] * 2 + [dma((n // 2 + 1) * SPLIT)] * 2,
         compiler_params=pltpu.CompilerParams(
-            collective_id=0, has_side_effects=True, vmem_limit_bytes=56 * 1024 * 1024
+            collective_id=0, has_side_effects=True, vmem_limit_bytes=60 * 1024 * 1024
         ),
     )(
         source, block_job, adapter_home, tokens, up_weight, adapter_a[0].T,
-        adapter_b.reshape(jobs * rank, hidden), cotangent,
+        factor_b, cotangent,
     )
+    mixed, grad_a, grad_b = pl.pallas_call(
+        finish,
+        out_shape=(
+            jax.ShapeDtypeStruct((rows, hidden), bf16),
+            jax.ShapeDtypeStruct((rank, width), f32),
+            jax.ShapeDtypeStruct((jobs * rank, hidden), f32),
+        ),
+        in_specs=[anywhere] * 5,
+        out_specs=(anywhere,) * 3,
+        scratch_shapes=[
+            pltpu.VMEM((rows, hidden), f32),
+            pltpu.VMEM((jobs * rank, rows), bf16),
+            pltpu.VMEM((jobs * rank, hidden), bf16),
+            pltpu.VMEM((rows, hidden), bf16),
+            pltpu.VMEM((rank, width), f32),
+            pltpu.VMEM((rows, hidden), bf16),
+            pltpu.VMEM((jobs * rank, hidden), f32),
+            dma(7 + OUT_PARTS),
+        ],
+        compiler_params=pltpu.CompilerParams(vmem_limit_bytes=60 * 1024 * 1024),
+    )(base, grad_a, codes, factor_b, cotangent)
     return mixed, grad_a.T[None], grad_b.reshape(jobs, rank, hidden)
 
 

time: 49 us -> 43.6 us (0.89)
  local copies, waits for them, and re-layouts: 5.05 us -> 0 us
    unnamed x5 -> x0, local copies, waits for them, and re-layouts: 5.05 us -> none
    pallas_call x1, Pallas kernels: 43.1 us -> 39.8 us  [on_device(): pl.pallas_call(functools.partial(kernel, n, rows_y, rank), out_shape=(jax...]
    pallas_call x0 -> x1, Pallas kernels: none -> 2.99 us  [on_device(): pl.pallas_call(finish, out_shape=(jax.ShapeDtypeStruct((rows, hidden), bf...]
where the time goes in v2:
time: 43.6 us; the launch traced here: 43.5 us
  Pallas kernels  42.8 us (98%)
  between operations  0.64 us (1%)
    pallas_call x1, Pallas kernels, on_device(): pl.pallas_call(functools.partial(kernel, n, rows_y, rank), out_shape=(jax...  39.8 us
    pallas_call x1, Pallas kernels, on_device(): pl.pallas_call(finish, out_shape=(jax.ShapeDtypeStruct((rows, hidden), bf...  2.99 us

profile of v2, /device:TPU:0, one launch (start us, length us, event | category | flops | bytes accessed | tf_op | source)
XLA Modules:
  0.0 43.5 jit_solution(17300535521102170888)
XLA Ops:
  0.6 39.8 %shard_map.103 = (f32[128,1792]{1,0:T(8,128)}, f32[16,8192]{1,0:T(8,128)}, bf16[256,128]{1,0:T(8,128)(2,1)}) custom-call(s32[16]{0:T(128)} %source.1, s32[48]{0:T(128)} %block_job.1, s32[16]{0:T(128)} %adapter_home.1, bf16[24,8192]{1,0:T(8,128)(2,1)} %tokens.1, bf16[8192,1792]{1,0:T(8,128)(2,1)} %up_weight.1, bf16[16,8192]{1,0:T(8,128)(2,1)} %bitcast.10, ...), custom_call_target="tpu_custom_call" | custom-call | tf_op jit(solution)/shard_map/pallas_call | solution.py:292
  40.5 3.0 %shard_map.104 = (bf16[128,1792]{1,0:T(8,128)(2,1)}, f32[16,8192]{1,0:T(8,128)}, f32[256,1792]{1,0:T(8,128)}) custom-call(f32[128,1792]{1,0:T(8,128)} %get-tuple-element.9.total_in, f32[16,8192]{1,0:T(8,128)} %get-tuple-element.10.grad_a_in, bf16[256,128]{1,0:T(8,128)(2,1)} %get-tuple-element.11.codes_in, bf16[256,1792]{1,0:T(8,128)(2,1)} %bitcast.9, ...), custom_call_target="tpu_custom_call" | custom-call | tf_op jit(solution)/shard_map/pallas_call | solution.py:325

commit v3 on v2

--- a/solution.py
+++ b/solution.py
@@ -135,10 +135,15 @@
         at, index = pl.ds(i * cut, cut), (2 * t + h) * SPLIT + i
         return remote(picked.at[k, at], picked.at[k, at], pair_send.at[index], pair_recv.at[index], sibling)
 
+    def use_base(k):
+        total[...] += dot(picked[k], weight[columns(k), :])
+
+    def use_code(k):
+        code_acc[...] += dot(factor_a[:, columns(k)], picked[k], ((1,), (1,)))
+
     def use(k):
-        part = picked[k]
-        total[...] += dot(part, weight[columns(k), :])
-        code_acc[...] += dot(factor_a[:, columns(k)], part, ((1,), (1,)))
+        use_base(k)
+        use_code(k)
 
     for i in range(SPLIT):
         pair(0, 0, i).start()
@@ -187,16 +192,20 @@
     for i in range(SPLIT):
         ring(half - 1, 0, i).wait_recv()
         pair(half, 0, i).start()
-    use(sibling if half == 1 else piece(half - 1, 1))
-    use(piece(half, 0))
+    late = [sibling if half == 1 else piece(half - 1, 1), piece(half, 0)]
+    for k in late:
+        use_code(k)
     if half > 1:
         for h in range(2):
             for i in range(SPLIT):
                 pair(half - 1, h, i).wait_recv()
-            use(piece(half - 1, 1 - h, 1))
+            late.append(piece(half - 1, 1 - h, 1))
+            use_code(late[-1])
+    use_base(late[0])
     for i in range(SPLIT):
         pair(half, 0, i).wait_recv()
-    use(piece(half, 1, 1))
+    late.append(piece(half, 1, 1))
+    use_code(late[-1])
 
     codes[me] = code_acc[...].astype(jnp.bfloat16)
 
@@ -206,6 +215,8 @@
 
     each(lambda offset: code_copy(offset).start())
 
+    for k in late[1:]:
+        use_base(k)
     store_total = local(total, total_out, 0)
     store_total.start()
     each_chip(lambda offset: back_copy(offset).wait_recv())

time: 43.6 us -> 42.6 us (0.977)
  Pallas kernels: 42.8 us -> 41.8 us
    pallas_call x1, Pallas kernels: 39.8 us -> 38.8 us  [on_device(): pl.pallas_call(functools.partial(kernel, n, rows_y, rank), out_shape=(jax...]
where the time goes in v3:
time: 42.6 us; the launch traced here: 42.4 us
  Pallas kernels  41.8 us (98%)
  between operations  0.64 us (2%)
    pallas_call x1, Pallas kernels, on_device(): pl.pallas_call(functools.partial(kernel, n, rows_y, rank), out_shape=(jax...  38.8 us
    pallas_call x1, Pallas kernels, on_device(): pl.pallas_call(finish, out_shape=(jax.ShapeDtypeStruct((rows, hidden), bf...  2.99 us

profile of v3, /device:TPU:0, one launch (start us, length us, event | category | flops | bytes accessed | tf_op | source)
XLA Modules:
  0.0 42.4 jit_solution(11686341132247556520)
XLA Ops:
  0.6 38.8 %shard_map.103 = (f32[128,1792]{1,0:T(8,128)}, f32[16,8192]{1,0:T(8,128)}, bf16[256,128]{1,0:T(8,128)(2,1)}) custom-call(s32[16]{0:T(128)} %source.1, s32[48]{0:T(128)} %block_job.1, s32[16]{0:T(128)} %adapter_home.1, bf16[24,8192]{1,0:T(8,128)(2,1)} %tokens.1, bf16[8192,1792]{1,0:T(8,128)(2,1)} %up_weight.1, bf16[16,8192]{1,0:T(8,128)(2,1)} %bitcast.10, ...), custom_call_target="tpu_custom_call" | custom-call | tf_op jit(solution)/shard_map/pallas_call | solution.py:303
  39.5 3.0 %shard_map.104 = (bf16[128,1792]{1,0:T(8,128)(2,1)}, f32[16,8192]{1,0:T(8,128)}, f32[256,1792]{1,0:T(8,128)}) custom-call(f32[128,1792]{1,0:T(8,128)} %get-tuple-element.9.total_in, f32[16,8192]{1,0:T(8,128)} %get-tuple-element.10.grad_a_in, bf16[256,128]{1,0:T(8,128)(2,1)} %get-tuple-element.11.codes_in, bf16[256,1792]{1,0:T(8,128)(2,1)} %bitcast.9, ...), custom_call_target="tpu_custom_call" | custom-call | tf_op jit(solution)/shard_map/pallas_call | solution.py:336
